TPU v7x, 32 devices: a whole 2x2x4 slice. The times are simulated.
32 devices in a mesh: ccd: 4 (over y, core), tile: 8 (over z, x).
Axes of the slice: x: 2, y: 2, z: 4, core: 2. Of those that a mesh axis runs over, the one named last changes fastest.
Arguments:
- exposures: float32 [8, 2048, 4096], P('tile', 'ccd'), may hold values from -6 to 6
- interp: bfloat16 [8, 32, 256, 128], P('tile'), may hold values from -0.375 to 0.375
- col_offsets: int32 [8, 32], P('tile'), may hold values from 0 to 30
- template: float32 [2048, 4096], P('ccd', 'tile'), may hold values from -6 to 6
- coef_table: float32 [8, 4, 3, 3], replicated, may hold values from -3 to 3
- coef_index: int32 [8, 4, 8], replicated, may hold values from 0 to 3
- intersection: int32 [8, 4, 8], replicated, may hold values 0 or 1
Outputs:
- difference: float32 [8, 2048, 4096], P('tile', 'ccd')
All inputs are finite; a program needn't handle non-finite values.
Results may differ from a plain program's by a relative error of at most 0.0029.
Values sent between devices are 32-bit elements; how exact they have to be, the bound alone decides.
A program may use at most 128 MiB of HBM per device.

v0:
```python
import jax
import jax.numpy as jnp
from jax import lax
from jax.sharding import PartitionSpec as P

HALF = 10
KSETS = 4
SIGMAS = (1.5, 3.0, 5.0)


def extended(array, sides, width):
    for axis, dim in sides:
        size, length = (lax.axis_size(axis), array.shape[dim])
        up = [(i, (i + 1) % size) for i in range(size - 1)]
        down = [(j, i) for i, j in up]
        last = lax.slice_in_dim(array, length - width, length, axis=dim)
        leading = lax.slice_in_dim(array, 0, width, axis=dim)
        before = lax.ppermute(last, axis, up)
        after = lax.ppermute(leading, axis, down)
        array = jnp.concatenate([before, array, after], axis=dim)
    return array


def basis_taps(half_width):
    positions = jnp.arange(-half_width, half_width + 1).astype(jnp.float32)
    kernels = []
    for sigma_value in SIGMAS:
        gauss = jnp.exp(-0.5 * (positions / sigma_value) ** 2)
        kernels.append(gauss / jnp.sum(gauss))
    return kernels


def smooth(padded, gauss, out_rows, out_cols):
    tap_count = gauss.shape[0]
    across = gauss[0] * padded[0:out_rows, :]
    for offset in range(1, tap_count):
        across = across + gauss[offset] * padded[offset : offset + out_rows, :]
    result = gauss[0] * across[:, 0:out_cols]
    for offset in range(1, tap_count):
        result = result + gauss[offset] * across[:, offset : offset + out_cols]
    return result


def resample(exposure_img, weights, offsets):
    row_count = exposure_img.shape[0]
    block_count = weights.shape[0]
    block_cols = weights.shape[2]
    tiles = exposure_img.astype(jnp.bfloat16).reshape(row_count, block_count, block_cols)
    first_part = jnp.take(tiles, offsets, axis=1)
    second_part = jnp.take(tiles, offsets + 1, axis=1)
    window = jnp.concatenate([first_part, second_part], axis=2)
    output = jnp.einsum("rjk,jkn->rjn", window, weights, preferred_element_type=jnp.float32)
    return output.reshape(row_count, block_count * block_cols)


def on_device(exposures, interp, col_offsets, template, coef_table, coef_index, intersection):
    row_count = exposures.shape[1]
    col_count = exposures.shape[2]
    patch_cols = template.shape[1]
    kernels = basis_taps(HALF)
    patch_row = lax.axis_index("ccd")
    my_epoch = lax.axis_index("tile")
    warped = resample(exposures[0], interp[0], col_offsets[0])
    row_coord = (jnp.arange(row_count).astype(jnp.float32) - (row_count - 1) / 2.0) / (
        row_count / 2.0
    )
    set_range = jnp.arange(KSETS)
    padded = extended(template, (("ccd", 0), ("tile", 1)), HALF)
    smoothed = [smooth(padded, gauss, row_count, patch_cols) for gauss in kernels]
    row_bases = (
        lax.all_gather(smoothed[0], "tile", axis=1, tiled=True),
        lax.all_gather(smoothed[1], "tile", axis=1, tiled=True),
        lax.all_gather(smoothed[2], "tile", axis=1, tiled=True),
    )
    set_ids = coef_index[my_epoch, patch_row]
    set_pick = (set_ids[:, None] == set_range[None, :]).astype(jnp.float32)
    kernel_coef = jnp.sum(set_pick[:, :, None, None] * coef_table[my_epoch][None], axis=1)
    column_coef = jnp.repeat(kernel_coef, patch_cols, axis=0)
    col_coord = (
        (jnp.arange(col_count) % patch_cols).astype(jnp.float32) - (patch_cols - 1) / 2.0
    ) / (patch_cols / 2.0)
    template_model = None
    for kernel_index in range(3):
        const_part = column_coef[:, kernel_index, 0][None, :]
        col_slope = column_coef[:, kernel_index, 1][None, :]
        row_slope = column_coef[:, kernel_index, 2][None, :]
        weight_map = const_part + col_slope * col_coord[None, :] + row_slope * row_coord[:, None]
        contrib = weight_map * row_bases[kernel_index]
        template_model = contrib if template_model is None else template_model + contrib
    coverage = jnp.repeat(intersection[my_epoch, patch_row].astype(jnp.float32), patch_cols)
    difference = (warped - template_model) * coverage[None, :]
    return difference[None]


def solution(mesh):
    placed = (
        P("tile", "ccd", None),
        P("tile", None, None, None),
        P("tile", None),
        P("ccd", "tile"),
        P(),
        P(),
        P(),
    )
    return jax.shard_map(
        on_device, mesh=mesh, in_specs=placed, out_specs=P("tile", "ccd", None), check_vma=False
    )
```

profile of v0, /device:TPU:0, one launch (start us, length us, event | category | flops | bytes accessed | tf_op | source)
XLA Modules:
  0.0 469.4 jit_solution(13398346818644322910)
XLA Ops:
  6.5 0.0 copy-start
  6.5 0.0 all-gather.8.cloned.1.call-start
  6.5 0.0 copy-start.1
  6.5 0.9 fusion.79
  7.5 1.4 collective-permute-start.1
  8.9 3.0 collective-permute-start
  11.9 0.6 fusion.77
  12.6 0.7 broadcast_divide_fusion
  13.2 0.7 fusion.85
  13.9 0.0 collective-permute-done.1
  13.9 0.0 collective-permute-done
  14.0 1.2 pad_maximum_fusion.3
  15.1 1.3 collective-permute-start.3
  16.4 5.5 %collective-permute-start.2 = (f32[532,10]{1,0:T(8,128)S(1)}, f32[532,10]{1,0:T(8,128)S(1)}, u32[]{:S(2)}, u32[]{:S(2)}) collective-permute-start(f32[532,10]{1,0:T(8,128)S(1)} %get-tuple-element.8), channel_id=1, source_target_pairs={{0,1},{1,2},{2,3},{3,4},{4,5},{5,6},{6,7},{8,9},{9,10},{10,11},{11... | collective-permute-start | bytes 63848 | tf_op jit(solution)/shard_map/ppermute | solution.py:18
  21.9 0.7 fusion.86
  22.6 4.2 collective-permute-done.3
  26.8 6.9 %collective-permute-done.2 = f32[532,10]{1,0:T(8,128)S(1)} collective-permute-done((f32[532,10]{1,0:T(8,128)S(1)}, f32[532,10]{1,0:T(8,128)S(1)}, u32[]{:S(2)}, u32[]{:S(2)}) %collective-permute-start.2) | collective-permute-done | bytes 21312 | tf_op jit(solution)/shard_map/ppermute | solution.py:18
  33.7 0.0 copy-done.1
  33.7 0.5 pad_maximum_fusion
  34.2 16.5 %multiply_add_fusion = f32[512,532]{1,0:T(8,128)S(1)} fusion(f32[532,532]{1,0:T(8,128)S(1)} %pad_maximum_fusion, f32[]{:T(128)} %bitcast.81, f32[]{:T(128)} %bitcast.80, f32[]{:T(128)} %bitcast.79, f32[]{:T(128)} %bitcast.78, f32[]{:T(128)} %bitcast.77, f32[]{:T(128)} %bitcast.76, f32[]{:T(128)} %bitcast.75, f32[]{:T(128)} %bitcast.74, f32[]{:T(128)} %bitcast.73, ...), kind=kLoop, calls=%fused_computation.11 | loop fusion | flops 11167744 | bytes 23969876 | tf_op jit(solution)/shard_map/add | solution.py:37
  50.7 19.6 %fusion.5 = f32[512,512]{1,0:T(8,128)} fusion(f32[512,532]{1,0:T(8,128)S(1)} %multiply_add_fusion, f32[]{:T(128)} %bitcast.81, f32[]{:T(128)} %bitcast.80, f32[]{:T(128)} %bitcast.79, f32[]{:T(128)} %bitcast.78, f32[]{:T(128)} %bitcast.77, f32[]{:T(128)} %bitcast.76, f32[]{:T(128)} %bitcast.75, f32[]{:T(128)} %bitcast.74, f32[]{:T(128)} %bitcast.73, ...), kind=kLoop, calls=%fused_computation.15 | loop fusion | flops 10747904 | bytes 23068756 | tf_op jit(solution)/shard_map/add | solution.py:40
  70.3 0.0 all-gather.8.cloned.1.call-update
  70.3 0.0 all-gather.6.cloned.1.call-start
  70.4 0.6 fusion.76
  71.0 0.7 broadcast_divide_fusion.1
  71.7 0.6 fusion.84
  72.3 0.7 fusion.83
  73.0 16.3 %multiply_add_fusion.1 = f32[512,532]{1,0:T(8,128)S(1)} fusion(f32[532,532]{1,0:T(8,128)S(1)} %pad_maximum_fusion, f32[]{:T(128)} %bitcast.57, f32[]{:T(128)} %bitcast.56, f32[]{:T(128)} %bitcast.55, f32[]{:T(128)} %bitcast.54, f32[]{:T(128)} %bitcast.53, f32[]{:T(128)} %bitcast.52, f32[]{:T(128)} %bitcast.51, f32[]{:T(128)} %bitcast.50, f32[]{:T(128)} %bitcast.49, ...), kind=kLoop, calls=%fused_computation.12 | loop fusion | flops 11167744 | bytes 23969876 | tf_op jit(solution)/shard_map/add | solution.py:37
  89.3 19.3 %fusion.25 = f32[512,512]{1,0:T(8,128)} fusion(f32[512,532]{1,0:T(8,128)S(1)} %multiply_add_fusion.1, f32[]{:T(128)} %bitcast.57, f32[]{:T(128)} %bitcast.56, f32[]{:T(128)} %bitcast.55, f32[]{:T(128)} %bitcast.54, f32[]{:T(128)} %bitcast.53, f32[]{:T(128)} %bitcast.52, f32[]{:T(128)} %bitcast.51, f32[]{:T(128)} %bitcast.50, f32[]{:T(128)} %bitcast.49, ...), kind=kLoop, calls=%fused_computation.56 | loop fusion | flops 10747904 | bytes 23068756 | tf_op jit(solution)/shard_map/add | solution.py:40
  108.5 0.0 all-gather.6.cloned.1.call-update
  108.6 0.2 all-gather.4.cloned.1.call-start
  108.8 0.6 fusion.75
  109.4 0.7 broadcast_divide_fusion.2
  110.1 0.7 fusion.82
  110.7 0.7 fusion.81
  111.5 16.5 %multiply_add_fusion.2 = f32[512,532]{1,0:T(8,128)S(1)} fusion(f32[532,532]{1,0:T(8,128)S(1)} %pad_maximum_fusion, f32[]{:T(128)} %bitcast.33, f32[]{:T(128)} %bitcast.32, f32[]{:T(128)} %bitcast.31, f32[]{:T(128)} %bitcast.30, f32[]{:T(128)} %bitcast.29, f32[]{:T(128)} %bitcast.28, f32[]{:T(128)} %bitcast.27, f32[]{:T(128)} %bitcast.26, f32[]{:T(128)} %bitcast.25, ...), kind=kLoop, calls=%fused_computation.13 | loop fusion | flops 11167744 | bytes 23969876 | tf_op jit(solution)/shard_map/add | solution.py:37
  128.0 19.6 %fusion.45 = f32[512,512]{1,0:T(8,128)} fusion(f32[512,532]{1,0:T(8,128)S(1)} %multiply_add_fusion.2, f32[]{:T(128)} %bitcast.33, f32[]{:T(128)} %bitcast.32, f32[]{:T(128)} %bitcast.31, f32[]{:T(128)} %bitcast.30, f32[]{:T(128)} %bitcast.29, f32[]{:T(128)} %bitcast.28, f32[]{:T(128)} %bitcast.27, f32[]{:T(128)} %bitcast.26, f32[]{:T(128)} %bitcast.25, ...), kind=kLoop, calls=%fused_computation.97 | loop fusion | flops 10747904 | bytes 23068756 | tf_op jit(solution)/shard_map/add | solution.py:40
  147.5 0.0 all-gather.4.cloned.1.call-update
  147.6 7.3 %copy.23 = bf16[1,512,4096]{1,2,0:T(8,128)(2,1)} copy(f32[1,512,4096]{2,1,0:T(8,128)} %param.9) | data formatting | bytes 12582912 | tf_op args[0]
  154.9 0.0 copy-start.3
  154.9 6.4 %copy.24 = bf16[512,32,128]{2,0,1:T(8,128)(2,1)} copy(bf16[512,32,128]{0,2,1:T(8,128)(2,1)} %bitcast.108) | data formatting | bytes 8388608 | tf_op jit(solution)/shard_map/convert_element_type | solution.py:48
  161.3 0.0 copy-done.3
  161.3 5.3 %gather_fusion.1 = bf16[32,512,128]{2,1,0:T(8,128)(2,1)} fusion(bf16[512,32,128]{2,0,1:T(8,128)(2,1)} %copy.24, s32[1024]{0:T(1024)S(1)} %pad_clamp_fusion), kind=kCustom, calls=%fused_computation.1.clone | custom fusion | bytes 8388736 | tf_op jit(solution)/shard_map/jit(_take)/gather | solution.py:50
  166.6 5.2 %gather_fusion = bf16[32,512,128]{2,1,0:T(8,128)(2,1)} fusion(bf16[512,32,128]{2,0,1:T(8,128)(2,1)} %copy.24, s32[1024]{0:T(1024)S(1)} %pad_clamp_fusion.1), kind=kCustom, calls=%fused_computation.clone | custom fusion | bytes 8388736 | tf_op jit(solution)/shard_map/jit(_take)/gather | solution.py:49
  171.9 5.2 %select_bitcast_fusion = (bf16[512,32,128]{2,0,1:T(8,128)(2,1)S(1)}, bf16[512,32,128]{2,0,1:T(8,128)(2,1)}) fusion(bf16[32,512,128]{2,1,0:T(8,128)(2,1)} %gather_fusion.1, pred[32]{0:T(512)(128)(4,1)S(1)} %get-tuple-element.6, bf16[32,512,128]{2,1,0:T(8,128)(2,1)} %gather_fusion, pred[32]{0:T(512)(128)(4,1)S(1)} %get-tuple-element.84), kind=kLoop, calls=%fused_computation.7 | loop fusion | flops 4194304 | bytes 16777280 | tf_op jit(solution)/shard_map/jit(_take)/select_n | solution.py:50
  177.1 0.0 copy-done
  177.1 8.5 %fusion = f32[32,512,128]{1,2,0:T(8,128)} fusion(bf16[512,32,128]{2,0,1:T(8,128)(2,1)S(1)} %get-tuple-element.87, bf16[512,32,128]{2,0,1:T(8,128)(2,1)} %get-tuple-element.88, bf16[1,32,256,128]{3,2,1,0:T(8,128)(2,1)S(1)} %copy-done), kind=kOutput, calls=%fused_computation.2 | convolution fusion | flops 1090519040 | bytes 18874368 | tf_op jit(solution)/shard_map/rjk,jkn->rjn/dot_general | solution.py:52
  185.6 0.0 copy-start.2
  185.6 8.9 %copy.29 = f32[512,4096]{1,0:T(8,128)} copy(f32[512,4096]{0,1:T(8,128)} %bitcast.107) | data formatting | bytes 16777216 | tf_op jit(solution)/shard_map/reshape | solution.py:53
  194.5 0.7 fusion.72
  195.2 0.1 broadcast_bitcast_fusion
  195.3 0.0 copy-done.2
  195.3 0.1 constant_dynamic-slice_fusion.1
  195.4 0.2 copy.31
  195.6 0.1 multiply_reduce_fusion
  195.7 0.1 broadcast_in_dim.15
  195.7 0.1 reshape.109
  195.9 0.1 fusion.80
  196.0 0.0 all-gather.8.cloned.1.call-done
  196.1 124.9 %all-gather.6.cloned.1.call-done = f32[512,4096]{1,0:T(8,128)} async-done(((f32[512,512]{1,0:T(8,128)}), f32[512,4096]{1,0:T(8,128)}) %all-gather.6.cloned.1.call-update) | async-done | bytes 8388624 | tf_op jit(solution)/shard_map/all_gather | solution.py:72
  321.0 125.3 %all-gather.4.cloned.1.call-done = f32[512,4096]{1,0:T(8,128)} async-done(((f32[512,512]{1,0:T(8,128)}), f32[512,4096]{1,0:T(8,128)}) %all-gather.4.cloned.1.call-update) | async-done | bytes 8388624 | tf_op jit(solution)/shard_map/all_gather | solution.py:71
  446.3 16.6 %multiply_bitcast_fusion = f32[1,512,4096]{2,1,0:T(8,128)} fusion(f32[512,4096]{1,0:T(8,128)} %copy.29, f32[512,4096]{1,0:T(8,128)} %all-gather.8.cloned.1.call-done, f32[512,4096]{1,0:T(8,128)} %all-gather.6.cloned.1.call-done, f32[512,4096]{1,0:T(8,128)} %all-gather.4.cloned.1.call-done, f32[4096]{0:T(1024)S(1)} %bitcast.112, f32[4096]{0:T(1024)S(1)} %bitcast.109, ...), kind=kLoop, calls=%fused_computation.6 | loop fusion | flops 27262976 | bytes 42059776 | tf_op jit(solution)/shard_map/broadcast_in_dim | solution.py:92
  (10 shorter events, 0.1 us)
Async XLA Ops:
  6.5 170.6 %copy-start = (bf16[1,32,256,128]{3,2,1,0:T(8,128)(2,1)S(1)}, bf16[1,32,256,128]{3,2,1,0:T(8,128)(2,1)}, u32[]{:S(2)}) copy-start(bf16[1,32,256,128]{3,2,1,0:T(8,128)(2,1)} %param.10) | copy-start | bytes 6291460
  6.5 189.5 %all-gather.8.cloned.1.call-start = ((), (), s32[]{:S(2)}) async-start(), calls=%async_computation.2 | async-start | bytes 9437184 | tf_op jit(solution)/shard_map/all_gather | solution.py:73
  6.5 27.1 %copy-start.1 = (f32[512,512]{1,0:T(8,128)S(1)}, f32[512,512]{1,0:T(8,128)}, u32[]{:S(2)}) copy-start(f32[512,512]{1,0:T(8,128)} %param.12) | copy-start | bytes 3145732
  7.5 6.5 %collective-permute-start.1 = (f32[10,512]{1,0:T(8,128)S(1)}, f32[10,512]{1,0:T(8,128)S(1)}, u32[]{:S(2)}, u32[]{:S(2)}) collective-permute-start(f32[10,512]{1,0:T(8,128)S(1)} %get-tuple-element.11), channel_id=1, source_target_pairs={{8,0},{16,8},{24,16},{9,1},{17,9},{25,17},{10,2},{18,10},{26,18},{... | collective-permute-start | bytes 61448 | tf_op jit(solution)/shard_map/ppermute | solution.py:19
  8.9 5.1 %collective-permute-start = (f32[10,512]{1,0:T(8,128)S(1)}, f32[10,512]{1,0:T(8,128)S(1)}, u32[]{:S(2)}, u32[]{:S(2)}) collective-permute-start(f32[10,512]{1,0:T(8,128)S(1)} %get-tuple-element.10), channel_id=1, source_target_pairs={{0,8},{8,16},{16,24},{1,9},{9,17},{17,25},{2,10},{10,18},{18,26},{... | collective-permute-start | bytes 61448 | tf_op jit(solution)/shard_map/ppermute | solution.py:18
  15.1 11.6 %collective-permute-start.3 = (f32[532,10]{1,0:T(8,128)S(1)}, f32[532,10]{1,0:T(8,128)S(1)}, u32[]{:S(2)}, u32[]{:S(2)}) collective-permute-start(f32[532,10]{1,0:T(8,128)S(1)} %get-tuple-element.9), channel_id=1, source_target_pairs={{1,0},{2,1},{3,2},{4,3},{5,4},{6,5},{7,6},{9,8},{10,9},{11,10},{12... | collective-permute-start | bytes 63848 | tf_op jit(solution)/shard_map/ppermute | solution.py:19
  16.4 17.2 %collective-permute-start.2 = (f32[532,10]{1,0:T(8,128)S(1)}, f32[532,10]{1,0:T(8,128)S(1)}, u32[]{:S(2)}, u32[]{:S(2)}) collective-permute-start(f32[532,10]{1,0:T(8,128)S(1)} %get-tuple-element.8), channel_id=1, source_target_pairs={{0,1},{1,2},{2,3},{3,4},{4,5},{5,6},{6,7},{8,9},{9,10},{10,11},{11... | collective-permute-start | bytes 63848 | tf_op jit(solution)/shard_map/ppermute | solution.py:18
  70.3 250.6 %all-gather.6.cloned.1.call-start = ((), (), s32[]{:S(2)}) async-start(), calls=%async_computation.1 | async-start | bytes 9437184 | tf_op jit(solution)/shard_map/all_gather | solution.py:72
  108.6 337.7 %all-gather.4.cloned.1.call-start = ((), (), s32[]{:S(2)}) async-start(), calls=%async_computation | async-start | bytes 9437184 | tf_op jit(solution)/shard_map/all_gather | solution.py:71
  154.9 6.4 %copy-start.3 = (s32[1,32]{1,0:T(1,128)S(1)}, s32[1,32]{1,0:T(1,128)}, u32[]{:S(2)}) copy-start(s32[1,32]{1,0:T(1,128)} %param.11) | copy-start | bytes 388
  185.6 9.7 %copy-start.2 = (f32[8,4,3,3]{0,1,3,2:T(4,128)S(1)}, f32[8,4,3,3]{0,1,3,2:T(4,128)}, u32[]{:S(2)}) copy-start(f32[8,4,3,3]{0,1,3,2:T(4,128)} %param.13) | copy-start | bytes 3460
Sparse Core Ops, SparseCore 0:
  70.5 125.1 all-gather.7
  197.8 123.0 all-gather.5
  323.2 123.0 all-gather.3
where the time goes:
time: 471 us; the launch traced here: 469 us
  waiting for transfers between devices  261 us (55%)
  other arithmetic  136 us (29%)
  local copies, waits for them, and re-layouts  38.8 us (8%)
  between operations  13.3 us (3%)
  starting transfers between devices  11.5 us (2%)
  matrix products  8.5 us (2%)
    all_gather x1, waiting for transfers between devices, on_device(): lax.all_gather(smoothed[0], 'tile', axis=1, tiled=True)  125 us
    all_gather x1, waiting for transfers between devices, on_device(): lax.all_gather(smoothed[1], 'tile', axis=1, tiled=True)  125 us
    add x3, other arithmetic, smooth(): result = result + gauss[offset] * across[:, offset:offset + out_cols]  58.4 us
    add x3, other arithmetic, smooth(): across = across + gauss[offset] * padded[offset:offset + out_rows, :]  49.3 us
    broadcast_in_dim x1, other arithmetic, on_device(): return difference[None]  16.6 us
  transfers between devices with their start and end apart: 7, of which 4 were waited for; matrix products, arithmetic and copies ran while one was open for 27% of the time, Pallas kernels for 0%

commit v1 on v0

--- a/solution.py
+++ b/solution.py
@@ -2,10 +2,28 @@
 import jax.numpy as jnp
 from jax import lax
 from jax.sharding import PartitionSpec as P
+from jax.lax import axis_index, axis_size, ppermute
 
 HALF = 10
 KSETS = 4
 SIGMAS = (1.5, 3.0, 5.0)
+
+
+def form_lines(block_here):
+    z = axis_size("tile")
+    even, y, g_now = (z, axis_index("tile"), block_here.shape[1])
+    then, v1 = (block_here, 1)
+    while v1 < even:
+        then = jnp.concatenate(
+            [
+                then,
+                ppermute(then, "tile", [(hop_no, (hop_no - v1) % even) for hop_no in range(even)]),
+            ],
+            axis=1,
+        )
+        v1 = 2 * v1
+    a_now = jnp.roll(then, y * g_now, axis=1)
+    return a_now
 
 
 def extended(array, sides, width):
@@ -68,7 +86,7 @@
     padded = extended(template, (("ccd", 0), ("tile", 1)), HALF)
     smoothed = [smooth(padded, gauss, row_count, patch_cols) for gauss in kernels]
     row_bases = (
-        lax.all_gather(smoothed[0], "tile", axis=1, tiled=True),
+        form_lines(smoothed[0]),
         lax.all_gather(smoothed[1], "tile", axis=1, tiled=True),
         lax.all_gather(smoothed[2], "tile", axis=1, tiled=True),
     )

time: 471 us -> 589 us (1.25)
  waiting for transfers between devices: 261 us -> 338 us
  local copies, waits for them, and re-layouts: 38.8 us -> 61.4 us
  starting transfers between devices: 11.5 us -> 23.3 us
  other arithmetic: 136 us -> 142 us
    ppermute x0 -> x3, waiting for transfers between devices: none -> 328 us  [form_lines(): ppermute(then, 'tile', [(hop_no, (hop_no - v1) % even) for hop_no in rang...]
    all_gather x1 -> x0, waiting for transfers between devices: 125 us -> none  [on_device(): lax.all_gather(smoothed[0], 'tile', axis=1, tiled=True)]
    all_gather x1, waiting for transfers between devices: 125 us -> 0.01 us  [on_device(): lax.all_gather(smoothed[1], 'tile', axis=1, tiled=True)]
    unnamed x0 -> x1, other arithmetic: none -> 19.4 us
    add x3 -> x2, other arithmetic: 58.4 us -> 39 us  [smooth(): result = result + gauss[offset] * across[:, offset:offset + out_cols]]
    unnamed x11 -> x21, local copies, waits for them, and re-layouts: 7.4 us -> 23.6 us
    ppermute x0 -> x3, starting transfers between devices: none -> 14.6 us  [form_lines(): ppermute(then, 'tile', [(hop_no, (hop_no - v1) % even) for hop_no in rang...]
  transfers between devices with their start and end apart: 7 -> 9, of which waited for: 4 -> 6; matrix products, arithmetic and copies ran while one was open for 27% -> 27% of each run, Pallas kernels for 0% -> 0%
where the time goes in v1:
time: 589 us; the launch traced here: 587 us
  waiting for transfers between devices  338 us (57%)
  other arithmetic  142 us (24%)
  local copies, waits for them, and re-layouts  61.4 us (10%)
  starting transfers between devices  23.3 us (4%)
  between operations  13.5 us (2%)
  matrix products  8.52 us (1%)
    ppermute x3, waiting for transfers between devices, form_lines(): ppermute(then, 'tile', [(hop_no, (hop_no - v1) % even) for hop_no in rang...  328 us
    add x3, other arithmetic, smooth(): across = across + gauss[offset] * padded[offset:offset + out_rows, :]  49.3 us
    add x2, other arithmetic, smooth(): result = result + gauss[offset] * across[:, offset:offset + out_cols]  39 us
    unnamed x21, local copies, waits for them, and re-layouts  23.6 us
    unnamed x1, other arithmetic  19.4 us
    broadcast_in_dim x1, other arithmetic, on_device(): return difference[None]  16.6 us
    ppermute x3, starting transfers between devices, form_lines(): ppermute(then, 'tile', [(hop_no, (hop_no - v1) % even) for hop_no in rang...  14.6 us
  transfers between devices with their start and end apart: 9, of which 6 were waited for; matrix products, arithmetic and copies ran while one was open for 27% of the time, Pallas kernels for 0%

profile of v1, /device:TPU:0, one launch (start us, length us, event | category | flops | bytes accessed | tf_op | source)
XLA Modules:
  0.0 587.1 jit_solution(6639155434162272977)
XLA Ops:
  6.5 0.9 fusion.80
  7.5 2.5 collective-permute-start
  10.0 1.3 collective-permute-start.1
  11.3 0.6 fusion.76
  11.9 0.7 broadcast_divide_fusion.1
  12.5 0.7 fusion.84
  13.3 1.9 collective-permute-done.1
  15.2 1.2 pad_maximum_fusion.5
  16.4 3.4 collective-permute-start.2
  19.8 1.3 collective-permute-start.3
  21.1 0.6 fusion.85
  21.7 3.3 collective-permute-done.2
  25.0 4.7 collective-permute-done.3
  29.7 0.5 pad_maximum_fusion.2
  30.2 16.5 %multiply_add_fusion.1 = f32[512,532]{1,0:T(8,128)S(1)} fusion(f32[532,532]{1,0:T(8,128)S(1)} %pad_maximum_fusion.2, f32[]{:T(128)} %bitcast.57, f32[]{:T(128)} %bitcast.56, f32[]{:T(128)} %bitcast.55, f32[]{:T(128)} %bitcast.54, f32[]{:T(128)} %bitcast.53, f32[]{:T(128)} %bitcast.52, f32[]{:T(128)} %bitcast.51, f32[]{:T(128)} %bitcast.50, f32[]{:T(128)} %bitcast.49, ...), kind=kLoop, calls=%fused_computation.14 | loop fusion | flops 11167744 | bytes 23969876 | tf_op jit(solution)/shard_map/add | solution.py:55
  46.7 19.5 %fusion.25 = f32[512,512]{1,0:T(8,128)} fusion(f32[512,532]{1,0:T(8,128)S(1)} %multiply_add_fusion.1, f32[]{:T(128)} %bitcast.57, f32[]{:T(128)} %bitcast.56, f32[]{:T(128)} %bitcast.55, f32[]{:T(128)} %bitcast.54, f32[]{:T(128)} %bitcast.53, f32[]{:T(128)} %bitcast.52, f32[]{:T(128)} %bitcast.51, f32[]{:T(128)} %bitcast.50, f32[]{:T(128)} %bitcast.49, ...), kind=kLoop, calls=%fused_computation.58 | loop fusion | flops 10747904 | bytes 23068756 | tf_op jit(solution)/shard_map/add | solution.py:58
  66.2 0.0 all-gather.3.cloned.1.call-update
  66.2 0.2 all-gather.5.cloned.1.call-start
  66.5 0.6 fusion.77
  67.1 0.7 broadcast_divide_fusion
  67.7 0.6 fusion.87
  68.3 0.7 fusion.86
  69.1 16.5 %multiply_add_fusion = f32[512,532]{1,0:T(8,128)S(1)} fusion(f32[532,532]{1,0:T(8,128)S(1)} %pad_maximum_fusion.2, f32[]{:T(128)} %bitcast.81, f32[]{:T(128)} %bitcast.80, f32[]{:T(128)} %bitcast.79, f32[]{:T(128)} %bitcast.78, f32[]{:T(128)} %bitcast.77, f32[]{:T(128)} %bitcast.76, f32[]{:T(128)} %bitcast.75, f32[]{:T(128)} %bitcast.74, f32[]{:T(128)} %bitcast.73, ...), kind=kLoop, calls=%fused_computation.13 | loop fusion | flops 11167744 | bytes 23969876 | tf_op jit(solution)/shard_map/add | solution.py:55
  85.5 19.5 %fusion.5 = f32[512,512]{1,0:T(8,128)} fusion(f32[512,532]{1,0:T(8,128)S(1)} %multiply_add_fusion, f32[]{:T(128)} %bitcast.81, f32[]{:T(128)} %bitcast.80, f32[]{:T(128)} %bitcast.79, f32[]{:T(128)} %bitcast.78, f32[]{:T(128)} %bitcast.77, f32[]{:T(128)} %bitcast.76, f32[]{:T(128)} %bitcast.75, f32[]{:T(128)} %bitcast.74, f32[]{:T(128)} %bitcast.73, ...), kind=kLoop, calls=%fused_computation.17 | loop fusion | flops 10747904 | bytes 23068756 | tf_op jit(solution)/shard_map/add | solution.py:58
  105.0 0.0 all-gather.5.cloned.1.call-update
  105.1 0.6 fusion.75
  105.7 0.7 broadcast_divide_fusion.2
  106.3 0.6 fusion.83
  107.0 0.7 fusion.82
  107.7 16.4 %multiply_add_fusion.2 = f32[512,532]{1,0:T(8,128)S(1)} fusion(f32[532,532]{1,0:T(8,128)S(1)} %pad_maximum_fusion.2, f32[]{:T(128)} %bitcast.33, f32[]{:T(128)} %bitcast.32, f32[]{:T(128)} %bitcast.31, f32[]{:T(128)} %bitcast.30, f32[]{:T(128)} %bitcast.29, f32[]{:T(128)} %bitcast.28, f32[]{:T(128)} %bitcast.27, f32[]{:T(128)} %bitcast.26, f32[]{:T(128)} %bitcast.25, ...), kind=kLoop, calls=%fused_computation.15 | loop fusion | flops 11167744 | bytes 23969876 | tf_op jit(solution)/shard_map/add | solution.py:55
  124.1 19.4 %constant_dynamic-update-slice_fusion.7 = (f32[512,8192]{1,0:T(8,128)}, f32[512,512]{1,0:T(8,128)S(1)}) fusion(f32[512,532]{1,0:T(8,128)S(1)} %multiply_add_fusion.2, f32[]{:T(128)} %bitcast.33, f32[]{:T(128)} %bitcast.32, f32[]{:T(128)} %bitcast.31, f32[]{:T(128)} %bitcast.30, f32[]{:T(128)} %bitcast.29, f32[]{:T(128)} %bitcast.28, f32[]{:T(128)} %bitcast.27, ...), kind=kLoop, calls=%fused_computation.154 | loop fusion | flops 10747903 | bytes 24117332
  143.6 7.3 %collective-permute-start.4 = (f32[512,512]{1,0:T(8,128)S(1)}, f32[512,512]{1,0:T(8,128)S(1)}, u32[]{:S(2)}, u32[]{:S(2)}) collective-permute-start(f32[512,512]{1,0:T(8,128)S(1)} %get-tuple-element.7), channel_id=1, source_target_pairs={{0,7},{1,0},{2,1},{3,2},{4,3},{5,4},{6,5},{7,6},{8,15},{9,8},{10,9... | collective-permute-start | bytes 3145736 | tf_op jit(solution)/shard_map/ppermute | solution.py:20
  150.8 40.0 %collective-permute-done.4 = f32[512,512]{1,0:T(8,128)S(1)} collective-permute-done((f32[512,512]{1,0:T(8,128)S(1)}, f32[512,512]{1,0:T(8,128)S(1)}, u32[]{:S(2)}, u32[]{:S(2)}) %collective-permute-start.4) | collective-permute-done | bytes 1048608 | tf_op jit(solution)/shard_map/ppermute | solution.py:20
  190.9 1.6 pad_maximum_fusion.1
  192.4 0.1 copy-done.1
  192.5 4.7 collective-permute-start.5
  197.3 0.1 constant_dynamic-slice_fusion.1
  197.4 0.2 copy.31
  197.5 0.7 fusion.72
  198.2 0.1 multiply_reduce_fusion
  198.3 0.7 broadcast_in_dim.15
  199.1 1.0 reshape.109
  200.1 58.9 %collective-permute-done.5 = f32[512,1024]{1,0:T(8,128)} collective-permute-done((f32[512,1024]{1,0:T(8,128)}, f32[512,1024]{1,0:T(8,128)}, u32[]{:S(2)}, u32[]{:S(2)}) %collective-permute-start.5) | collective-permute-done | bytes 2097184 | tf_op jit(solution)/shard_map/ppermute | solution.py:20
  259.0 4.3 pad_maximum_fusion
  263.3 2.6 collective-permute-start.6
  265.9 0.1 broadcast_bitcast_fusion
  266.0 7.4 %copy.23 = bf16[1,512,4096]{1,2,0:T(8,128)(2,1)} copy(f32[1,512,4096]{2,1,0:T(8,128)} %param.9) | data formatting | bytes 12582912 | tf_op args[0]
  273.4 6.6 %copy.24 = bf16[512,32,128]{2,0,1:T(8,128)(2,1)} copy(bf16[512,32,128]{0,2,1:T(8,128)(2,1)} %bitcast.108) | data formatting | bytes 8388608 | tf_op jit(solution)/shard_map/convert_element_type | solution.py:66
  280.0 5.3 gather_fusion.1
  285.3 5.2 gather_fusion
  290.6 5.3 select_bitcast_fusion
  295.8 8.5 %fusion = f32[32,512,128]{1,2,0:T(8,128)} fusion(bf16[512,32,128]{2,0,1:T(8,128)(2,1)S(1)} %get-tuple-element.89, bf16[512,32,128]{2,0,1:T(8,128)(2,1)} %get-tuple-element.90, bf16[1,32,256,128]{3,2,1,0:T(8,128)(2,1)S(1)} %copy-done), kind=kOutput, calls=%fused_computation.2 | convolution fusion | flops 1090519040 | bytes 18874368 | tf_op jit(solution)/shard_map/rjk,jkn->rjn/dot_general | solution.py:70
  304.4 8.9 %copy.29 = f32[512,4096]{1,0:T(8,128)} copy(f32[512,4096]{0,1:T(8,128)} %bitcast.107) | data formatting | bytes 16777216 | tf_op jit(solution)/shard_map/reshape | solution.py:71
  313.3 0.1 fusion.81
  313.5 2.3 constant_dynamic-update-slice_fusion.6
  315.8 3.2 constant_dynamic-update-slice_fusion.5
  319.0 229.5 %collective-permute-done.6 = f32[512,2048]{1,0:T(8,128)} collective-permute-done((f32[512,2048]{1,0:T(8,128)}, f32[512,2048]{1,0:T(8,128)}, u32[]{:S(2)}, u32[]{:S(2)}) %collective-permute-start.6) | collective-permute-done | bytes 4194336 | tf_op jit(solution)/shard_map/ppermute | solution.py:20
  548.4 4.6 constant_dynamic-update-slice_fusion.4
  553.0 1.0 constant_dynamic-update-slice_fusion.3
  554.1 0.6 copy-done.2
  554.6 1.1 constant_dynamic-update-slice_fusion.2
  555.7 3.2 constant_dynamic-update-slice_fusion.1
  558.9 4.7 constant_dynamic-update-slice_fusion
  563.6 16.6 %multiply_bitcast_fusion = f32[1,512,4096]{2,1,0:T(8,128)} fusion(f32[512,4096]{1,0:T(8,128)} %copy.29, f32[512,4096]{1,0:T(8,128)} %all-gather.5.cloned.1.call-done, f32[512,4096]{1,0:T(8,128)} %all-gather.3.cloned.1.call-done, f32[512,8192]{1,0:T(8,128)} %constant_dynamic-update-slice_fusion, s32[]{:T(128)S(6)} %select_n.53, f32[4096]{0:T(1024)S(1)} %bitcast.112, ...), kind=kLoop, calls=%fused_computation.6 | loop fusion | flops 27262976 | bytes 42059780 | tf_op jit(solution)/shard_map/broadcast_in_dim | solution.py:110
  (24 shorter events, 0.1 us)
Async XLA Ops:
  6.5 289.3 %copy-start = (bf16[1,32,256,128]{3,2,1,0:T(8,128)(2,1)S(1)}, bf16[1,32,256,128]{3,2,1,0:T(8,128)(2,1)}, u32[]{:S(2)}) copy-start(bf16[1,32,256,128]{3,2,1,0:T(8,128)(2,1)} %param.10) | copy-start | bytes 6291460
  6.5 557.1 %all-gather.3.cloned.1.call-start = ((), (), s32[]{:S(2)}) async-start(), calls=%async_computation | async-start | bytes 9437184 | tf_op jit(solution)/shard_map/all_gather | solution.py:90
  6.5 23.2 %copy-start.3 = (f32[512,512]{1,0:T(8,128)S(1)}, f32[512,512]{1,0:T(8,128)}, u32[]{:S(2)}) copy-start(f32[512,512]{1,0:T(8,128)} %param.12) | copy-start | bytes 3145732
  7.5 5.8 collective-permute-start
  10.0 5.2 collective-permute-start.1
  16.4 8.6 %collective-permute-start.2 = (f32[532,10]{1,0:T(8,128)S(1)}, f32[532,10]{1,0:T(8,128)S(1)}, u32[]{:S(2)}, u32[]{:S(2)}) collective-permute-start(f32[532,10]{1,0:T(8,128)S(1)} %get-tuple-element.10), channel_id=1, source_target_pairs={{0,1},{1,2},{2,3},{3,4},{4,5},{5,6},{6,7},{8,9},{9,10},{10,11},{11... | collective-permute-start | bytes 63848 | tf_op jit(solution)/shard_map/ppermute | solution.py:36
  19.8 9.9 %collective-permute-start.3 = (f32[532,10]{1,0:T(8,128)S(1)}, f32[532,10]{1,0:T(8,128)S(1)}, u32[]{:S(2)}, u32[]{:S(2)}) collective-permute-start(f32[532,10]{1,0:T(8,128)S(1)} %get-tuple-element.11), channel_id=1, source_target_pairs={{1,0},{2,1},{3,2},{4,3},{5,4},{6,5},{7,6},{9,8},{10,9},{11,10},{12... | collective-permute-start | bytes 63848 | tf_op jit(solution)/shard_map/ppermute | solution.py:37
  66.2 497.4 %all-gather.5.cloned.1.call-start = ((), (), s32[]{:S(2)}) async-start(), calls=%async_computation.1 | async-start | bytes 9437184 | tf_op jit(solution)/shard_map/all_gather | solution.py:91
  143.6 53.7 %copy-start.4 = (f32[8,4,3,3]{0,1,3,2:T(4,128)S(1)}, f32[8,4,3,3]{0,1,3,2:T(4,128)}, u32[]{:S(2)}) copy-start(f32[8,4,3,3]{0,1,3,2:T(4,128)} %param.13) | copy-start | bytes 3460
  143.6 47.3 %collective-permute-start.4 = (f32[512,512]{1,0:T(8,128)S(1)}, f32[512,512]{1,0:T(8,128)S(1)}, u32[]{:S(2)}, u32[]{:S(2)}) collective-permute-start(f32[512,512]{1,0:T(8,128)S(1)} %get-tuple-element.7), channel_id=1, source_target_pairs={{0,7},{1,0},{2,1},{3,2},{4,3},{5,4},{6,5},{7,6},{8,15},{9,8},{10,9... | collective-permute-start | bytes 3145736 | tf_op jit(solution)/shard_map/ppermute | solution.py:20
  190.9 1.7 copy-start.1
  192.5 66.5 %collective-permute-start.5 = (f32[512,1024]{1,0:T(8,128)}, f32[512,1024]{1,0:T(8,128)}, u32[]{:S(2)}, u32[]{:S(2)}) collective-permute-start(f32[512,1024]{1,0:T(8,128)} %pad_maximum_fusion.1), channel_id=1, source_target_pairs={{0,6},{1,7},{2,0},{3,1},{4,2},{5,3},{6,4},{7,5},{8,14},{9,15},{10,... | collective-permute-start | bytes 6291464 | tf_op jit(solution)/shard_map/ppermute | solution.py:20
  263.3 285.1 %collective-permute-start.6 = (f32[512,2048]{1,0:T(8,128)}, f32[512,2048]{1,0:T(8,128)}, u32[]{:S(2)}, u32[]{:S(2)}) collective-permute-start(f32[512,2048]{1,0:T(8,128)} %pad_maximum_fusion), channel_id=1, source_target_pairs={{0,4},{1,5},{2,6},{3,7},{4,0},{5,1},{6,2},{7,3},{8,12},{9,13},{10,... | collective-permute-start | bytes 12582920 | tf_op jit(solution)/shard_map/ppermute | solution.py:20
  273.4 6.6 %copy-start.5 = (s32[1,32]{1,0:T(1,128)S(1)}, s32[1,32]{1,0:T(1,128)}, u32[]{:S(2)}) copy-start(s32[1,32]{1,0:T(1,128)} %param.11) | copy-start | bytes 388
  553.0 1.6 copy-start.2
Sparse Core Ops, SparseCore 0:
  66.3 162.6 all-gather.2
  231.3 286.1 all-gather.4
